TPU v7x, 32 devices: a whole 2x2x4 slice. The times are simulated.
32 devices in a mesh: seq: 4 (over y, core), wide: 8 (over z, x).
Axes of the slice: x: 2, y: 2, z: 4, core: 2. Of those that a mesh axis runs over, the one named last changes fastest.
Arguments:
- tokens: bfloat16 [2, 2048, 1152], P(None, ('seq', 'wide')), may hold values from -6 to 6
- out_grad: bfloat16 [2, 2048, 1152], P(None, ('seq', 'wide')), may hold values from -6 to 6
- norm_attn: bfloat16 [1152], P(('seq', 'wide')), may hold values from 0.25 to 1.75
- w_query: bfloat16 [1152, 1024], P(('seq', 'wide')), may hold values from -0.1875 to 0.1875
- w_key: bfloat16 [1152, 256], P(('seq', 'wide')), may hold values from -0.1875 to 0.1875
- w_value: bfloat16 [1152, 256], P(('seq', 'wide')), may hold values from -0.1875 to 0.1875
- norm_query: bfloat16 [256], P(('seq', 'wide')), may hold values from 0.25 to 1.75
- norm_key: bfloat16 [256], P(('seq', 'wide')), may hold values from 0.25 to 1.75
- w_output: bfloat16 [1024, 1152], P(('seq', 'wide')), may hold values from -0.1875 to 0.1875
- norm_attn_post: bfloat16 [1152], P(('seq', 'wide')), may hold values from 0.25 to 1.75
- norm_ffw: bfloat16 [1152], P(('seq', 'wide')), may hold values from 0.25 to 1.75
- w_gate: bfloat16 [1152, 6912], P(('seq', 'wide')), may hold values from -0.1875 to 0.1875
- w_up: bfloat16 [1152, 6912], P(('seq', 'wide')), may hold values from -0.1875 to 0.1875
- w_down: bfloat16 [6912, 1152], P(('seq', 'wide')), may hold values from -0.078125 to 0.078125
- norm_ffw_post: bfloat16 [1152], P(('seq', 'wide')), may hold values from 0.25 to 1.75
Outputs:
- layer_out: bfloat16 [2, 2048, 1152], P(None, ('seq', 'wide'))
- input_grad: float32 [2, 2048, 1152], P(None, ('seq', 'wide'))
- grad_norm_attn: float32 [1152], P(('seq', 'wide'))
- grad_w_query: float32 [1152, 1024], P(('seq', 'wide'))
- grad_w_key: float32 [1152, 256], P(('seq', 'wide'))
- grad_w_value: float32 [1152, 256], P(('seq', 'wide'))
- grad_norm_query: float32 [256], P(('seq', 'wide'))
- grad_norm_key: float32 [256], P(('seq', 'wide'))
- grad_w_output: float32 [1024, 1152], P(('seq', 'wide'))
- grad_norm_attn_post: float32 [1152], P(('seq', 'wide'))
- grad_norm_ffw: float32 [1152], P(('seq', 'wide'))
- grad_w_gate: float32 [1152, 6912], P(('seq', 'wide'))
- grad_w_up: float32 [1152, 6912], P(('seq', 'wide'))
- grad_w_down: float32 [6912, 1152], P(('seq', 'wide'))
- grad_norm_ffw_post: float32 [1152], P(('seq', 'wide'))
All inputs are finite; a program needn't handle non-finite values.
Results may differ from a plain program's by a relative error of at most 0.024.
Values may be sent and summed in bfloat16 or wider, within the bound.
A program may use at most 384 MiB of HBM per device.

v0:
```python
import jax
import jax.numpy as jnp
from jax import lax
from jax.sharding import PartitionSpec as P

EPSILON = 1e-06
ROPE_BASE = 1000000.0
SCORE_SCALE = 0.0625
MASKED = -1e30


def root_norm(values, gain_vector):
    return (
        values
        * lax.rsqrt(jnp.mean(values * values, axis=-1, keepdims=True) + EPSILON)
        * gain_vector
    )


def rotation(positions, width):
    half_width = width // 2
    frequency = ROPE_BASE ** (-2.0 * jnp.arange(half_width).astype(jnp.float32) / width)
    angles = positions.astype(jnp.float32)[:, None] * frequency[None, :]
    return (jnp.cos(angles), jnp.sin(angles))


def rotate(values, cosine, sine_table):
    half_width = values.shape[-1] // 2
    first_half = values[..., :half_width]
    second_half = values[..., half_width:]
    return jnp.concatenate(
        [
            first_half * cosine - second_half * sine_table,
            second_half * cosine + first_half * sine_table,
        ],
        axis=-1,
    )


def masked_scores(query_block, key_block, allowed):
    scores = (
        jnp.einsum("qd,kd->qk", query_block, key_block, preferred_element_type=jnp.float32)
        * SCORE_SCALE
    )
    return jnp.where(allowed, scores, MASKED)


def gelu_gate(gate_in, up_in):
    return jax.nn.gelu(gate_in, approximate=True) * up_in


def row_product(left, right):
    return jnp.einsum("snd,snc->dc", left, right, preferred_element_type=jnp.float32)


def on_device(
    tokens,
    out_grad,
    norm_attn,
    w_query,
    w_key,
    w_value,
    norm_query,
    norm_key,
    w_output,
    norm_attn_post,
    norm_ffw,
    w_gate,
    w_up,
    w_down,
    norm_ffw_post,
):
    seqs_here = tokens.shape[0]
    seq_rows = tokens.shape[1]
    heads = lax.axis_size("seq")
    wide_size = lax.axis_size("wide")
    head_dim = w_key.shape[1]
    gathered = (
        lax.all_gather(norm_attn, ("seq", "wide"), axis=0, tiled=True),
        lax.all_gather(w_query, ("seq", "wide"), axis=0, tiled=True),
        lax.all_gather(w_key, ("seq", "wide"), axis=0, tiled=True),
        lax.all_gather(w_value, ("seq", "wide"), axis=0, tiled=True),
        lax.all_gather(norm_query, ("seq", "wide"), axis=0, tiled=True),
        lax.all_gather(norm_key, ("seq", "wide"), axis=0, tiled=True),
        lax.all_gather(w_output, ("seq", "wide"), axis=0, tiled=True),
        lax.all_gather(norm_attn_post, ("seq", "wide"), axis=0, tiled=True),
        lax.all_gather(norm_ffw, ("seq", "wide"), axis=0, tiled=True),
        lax.all_gather(w_gate, ("seq", "wide"), axis=0, tiled=True),
        lax.all_gather(w_up, ("seq", "wide"), axis=0, tiled=True),
        lax.all_gather(w_down, ("seq", "wide"), axis=0, tiled=True),
        lax.all_gather(norm_ffw_post, ("seq", "wide"), axis=0, tiled=True),
    )
    (
        gain_attn,
        query_weight,
        key_weight,
        value_weight,
        gain_query,
        gain_key,
        output_weight,
        gain_attn_post,
        gain_ffw,
        gate_weight,
        up_weight,
        down_weight,
        gain_ffw_post,
    ) = gathered
    hidden_units = gate_weight.shape[1]
    query_width = query_weight.shape[1]
    block_index = lax.axis_index("seq") * wide_size + lax.axis_index("wide")
    local_pos = block_index * seq_rows + jnp.arange(seq_rows, dtype=jnp.int32)
    cosine, sine_table = rotation(local_pos, head_dim)

    def query_side(raw_values, gain_vector):
        return rotate(
            root_norm(raw_values, gain_vector), cosine[:, None, :], sine_table[:, None, :]
        )

    def key_side(raw_values, gain_vector):
        return rotate(root_norm(raw_values, gain_vector), cosine, sine_table)

    layer_in = tokens.astype(jnp.float32)
    normed_f, attn_in_pull = jax.vjp(root_norm, layer_in, gain_attn.astype(jnp.float32))
    normed = normed_f.astype(jnp.bfloat16)
    query_raw = jnp.dot(normed, query_weight, preferred_element_type=jnp.float32).reshape(
        seqs_here, seq_rows, heads, head_dim
    )
    key_raw = jnp.dot(normed, key_weight, preferred_element_type=jnp.float32)
    value_raw = jnp.dot(normed, value_weight, preferred_element_type=jnp.float32)
    query_shaped, query_pull = jax.vjp(query_side, query_raw, gain_query.astype(jnp.float32))
    key_shaped, key_pull = jax.vjp(key_side, key_raw, gain_key.astype(jnp.float32))
    queries = query_shaped.astype(jnp.bfloat16)
    keys_own = key_shaped.astype(jnp.bfloat16)
    values_own = value_raw.astype(jnp.bfloat16)
    head_rows = lax.all_to_all(queries, "seq", split_axis=2, concat_axis=1, tiled=True).reshape(
        seqs_here, heads * seq_rows, head_dim
    )
    all_keys, all_values = (
        lax.all_gather(keys_own, ("seq", "wide"), axis=1, tiled=True),
        lax.all_gather(values_own, ("seq", "wide"), axis=1, tiled=True),
    )
    total_len = all_keys.shape[1]
    row_ids = jnp.arange(heads * seq_rows, dtype=jnp.int32)
    query_pos = (
        row_ids // seq_rows * wide_size + lax.axis_index("wide")
    ) * seq_rows + row_ids % seq_rows
    key_pos = jnp.arange(total_len, dtype=jnp.int32)
    allowed = key_pos[None, :] <= query_pos[:, None]

    def attend_forward(operands):
        query_block, key_block, value_block = operands
        scores = masked_scores(query_block, key_block, allowed)
        peak = jnp.max(scores, axis=-1, keepdims=True)
        exponent = jnp.exp(scores - peak)
        total = jnp.sum(exponent, axis=-1, keepdims=True)
        probabilities = (exponent / total).astype(jnp.bfloat16)
        attended = jnp.dot(probabilities, value_block, preferred_element_type=jnp.float32)
        return (attended, (peak + jnp.log(total))[:, 0])

    attended, log_totals = lax.map(attend_forward, (head_rows, all_keys, all_values))
    attended_low = attended.astype(jnp.bfloat16).reshape(seqs_here, heads * seq_rows, 1, head_dim)
    token_heads = lax.all_to_all(
        attended_low, "seq", split_axis=1, concat_axis=2, tiled=True
    ).reshape(seqs_here, seq_rows, heads * head_dim)
    branch = jnp.dot(token_heads, output_weight, preferred_element_type=jnp.float32)
    branch_normed, attn_post_pull = jax.vjp(root_norm, branch, gain_attn_post.astype(jnp.float32))
    mixed = layer_in + branch_normed
    normed_ffw_f, ffw_in_pull = jax.vjp(root_norm, mixed, gain_ffw.astype(jnp.float32))
    normed_ffw = normed_ffw_f.astype(jnp.bfloat16)
    gate = jnp.dot(normed_ffw, gate_weight, preferred_element_type=jnp.float32)
    upward = jnp.dot(normed_ffw, up_weight, preferred_element_type=jnp.float32)
    middle_f, middle_pull = jax.vjp(gelu_gate, gate, upward)
    middle = middle_f.astype(jnp.bfloat16)
    output_raw = jnp.dot(middle, down_weight, preferred_element_type=jnp.float32)
    output_normed, ffw_post_pull = jax.vjp(root_norm, output_raw, gain_ffw_post.astype(jnp.float32))
    layer_out = (mixed + output_normed).astype(jnp.bfloat16)
    query_weight, key_weight, value_weight, output_weight, gate_weight, up_weight, down_weight = (
        lax.all_gather(w_query, ("seq", "wide"), axis=0, tiled=True),
        lax.all_gather(w_key, ("seq", "wide"), axis=0, tiled=True),
        lax.all_gather(w_value, ("seq", "wide"), axis=0, tiled=True),
        lax.all_gather(w_output, ("seq", "wide"), axis=0, tiled=True),
        lax.all_gather(w_gate, ("seq", "wide"), axis=0, tiled=True),
        lax.all_gather(w_up, ("seq", "wide"), axis=0, tiled=True),
        lax.all_gather(w_down, ("seq", "wide"), axis=0, tiled=True),
    )
    upstream = out_grad.astype(jnp.float32)
    d_output_f, grad_ffw_post = ffw_post_pull(upstream)
    d_output = d_output_f.astype(jnp.bfloat16)
    d_middle = jnp.einsum("snd,fd->snf", d_output, down_weight, preferred_element_type=jnp.float32)
    d_gate_f, d_up_f = middle_pull(d_middle)
    d_gate = d_gate_f.astype(jnp.bfloat16)
    d_up = d_up_f.astype(jnp.bfloat16)
    d_normed_ffw = jnp.einsum(
        "snf,df->snd", d_gate, gate_weight, preferred_element_type=jnp.float32
    ) + jnp.einsum("snf,df->snd", d_up, up_weight, preferred_element_type=jnp.float32)
    d_mixed_part, grad_ffw = ffw_in_pull(d_normed_ffw)
    d_mixed = upstream + d_mixed_part
    d_branch_f, grad_attn_post = attn_post_pull(d_mixed)
    d_branch = d_branch_f.astype(jnp.bfloat16)
    d_attended = jnp.einsum(
        "snd,cd->snc", d_branch, output_weight, preferred_element_type=jnp.float32
    ).astype(jnp.bfloat16)
    d_attended = d_attended.reshape(seqs_here, seq_rows, heads, head_dim)
    grad_heads = lax.all_to_all(d_attended, "seq", split_axis=2, concat_axis=1, tiled=True).reshape(
        seqs_here, heads * seq_rows, head_dim
    )

    def backward_tail(query_block, key_block, value_block, grad_block, log_block):
        scores = masked_scores(query_block, key_block, allowed)
        probabilities = jnp.exp(scores - log_block[:, None])
        prob_low = probabilities.astype(jnp.bfloat16)
        grad_values = jnp.einsum(
            "qk,qd->kd", prob_low, grad_block, preferred_element_type=jnp.float32
        )
        grad_probs = jnp.einsum(
            "qd,kd->qk", grad_block, value_block, preferred_element_type=jnp.float32
        )
        centre = jnp.sum(probabilities * grad_probs, axis=-1, keepdims=True)
        grad_scores = (probabilities * (grad_probs - centre)).astype(jnp.bfloat16)
        grad_query = (
            jnp.dot(grad_scores, key_block, preferred_element_type=jnp.float32) * SCORE_SCALE
        )
        grad_keys = (
            jnp.einsum("qk,qd->kd", grad_scores, query_block, preferred_element_type=jnp.float32)
            * SCORE_SCALE
        )
        own_keys, own_values = (
            lax.psum_scatter(grad_keys, ("seq", "wide"), scatter_dimension=0, tiled=True),
            lax.psum_scatter(grad_values, ("seq", "wide"), scatter_dimension=0, tiled=True),
        )
        return (grad_query, own_keys, own_values)

    def backward_sequence(operands):
        query_block, key_block, value_block, grad_block, log_block = operands
        return backward_tail(query_block, key_block, value_block, grad_block, log_block)

    sources = (head_rows, all_keys, all_values, grad_heads, log_totals)
    grad_query_rows, d_keys, d_values = lax.map(backward_sequence, sources)
    grad_query_rows = grad_query_rows.reshape(seqs_here, heads * seq_rows, 1, head_dim)
    d_queries = lax.all_to_all(
        grad_query_rows.astype(jnp.bfloat16), "seq", split_axis=1, concat_axis=2, tiled=True
    ).astype(grad_query_rows.dtype)
    d_query_raw_f, grad_gain_query = query_pull(d_queries)
    d_key_raw_f, grad_gain_key = key_pull(d_keys)
    d_query_raw = d_query_raw_f.reshape(seqs_here, seq_rows, heads * head_dim).astype(jnp.bfloat16)
    d_key_raw = d_key_raw_f.astype(jnp.bfloat16)
    d_value_raw = d_values.astype(jnp.bfloat16)
    d_normed = (
        jnp.einsum("snc,dc->snd", d_query_raw, query_weight, preferred_element_type=jnp.float32)
        + jnp.einsum("snc,dc->snd", d_key_raw, key_weight, preferred_element_type=jnp.float32)
        + jnp.einsum("snc,dc->snd", d_value_raw, value_weight, preferred_element_type=jnp.float32)
    )
    d_input_part, grad_attn = attn_in_pull(d_normed)
    input_grad = d_mixed + d_input_part
    input_side = lax.psum_scatter(
        jnp.concatenate(
            [
                row_product(normed, d_query_raw),
                row_product(normed, d_key_raw),
                row_product(normed, d_value_raw),
                row_product(normed_ffw, d_gate),
                row_product(normed_ffw, d_up),
            ],
            axis=1,
        ),
        ("seq", "wide"),
        scatter_dimension=0,
        tiled=True,
    )
    grad_output = lax.psum_scatter(
        row_product(token_heads, d_branch), ("seq", "wide"), scatter_dimension=0, tiled=True
    )
    grad_down = lax.psum_scatter(
        row_product(middle, d_output), ("seq", "wide"), scatter_dimension=0, tiled=True
    )
    edge_key = query_width + head_dim
    edge_value = edge_key + head_dim
    edge_gate = edge_value + hidden_units
    grad_query_w = input_side[:, :query_width]
    grad_key_w = input_side[:, query_width:edge_key]
    grad_value_w = input_side[:, edge_key:edge_value]
    grad_gate = input_side[:, edge_value:edge_gate]
    grad_upward = input_side[:, edge_gate:]
    gains = (
        lax.psum_scatter(grad_attn, ("seq", "wide"), scatter_dimension=0, tiled=True),
        lax.psum_scatter(grad_gain_query, ("seq", "wide"), scatter_dimension=0, tiled=True),
        lax.psum_scatter(grad_gain_key, ("seq", "wide"), scatter_dimension=0, tiled=True),
        lax.psum_scatter(grad_attn_post, ("seq", "wide"), scatter_dimension=0, tiled=True),
        lax.psum_scatter(grad_ffw, ("seq", "wide"), scatter_dimension=0, tiled=True),
        lax.psum_scatter(grad_ffw_post, ("seq", "wide"), scatter_dimension=0, tiled=True),
    )
    return (
        layer_out,
        input_grad,
        gains[0],
        grad_query_w,
        grad_key_w,
        grad_value_w,
        gains[1],
        gains[2],
        grad_output,
        gains[3],
        gains[4],
        grad_gate,
        grad_upward,
        grad_down,
        gains[5],
    )


def solution(mesh):
    placed = (
        P(None, ("seq", "wide"), None),
        P(None, ("seq", "wide"), None),
        P(("seq", "wide")),
        P(("seq", "wide"), None),
        P(("seq", "wide"), None),
        P(("seq", "wide"), None),
        P(("seq", "wide")),
        P(("seq", "wide")),
        P(("seq", "wide"), None),
        P(("seq", "wide")),
        P(("seq", "wide")),
        P(("seq", "wide"), None),
        P(("seq", "wide"), None),
        P(("seq", "wide"), None),
        P(("seq", "wide")),
    )
    return jax.shard_map(
        on_device,
        mesh=mesh,
        in_specs=placed,
        out_specs=(
            P(None, ("seq", "wide"), None),
            P(None, ("seq", "wide"), None),
            P(("seq", "wide")),
            P(("seq", "wide"), None),
            P(("seq", "wide"), None),
            P(("seq", "wide"), None),
            P(("seq", "wide")),
            P(("seq", "wide")),
            P(("seq", "wide"), None),
            P(("seq", "wide")),
            P(("seq", "wide")),
            P(("seq", "wide"), None),
            P(("seq", "wide"), None),
            P(("seq", "wide"), None),
            P(("seq", "wide")),
        ),
        check_vma=False,
    )
```

profile of v0, /device:TPU:0, one launch (start us, length us, event | category | flops | bytes accessed | tf_op | source)
XLA Modules:
  0.0 2779.5 jit_solution(733972483307430903)
XLA Ops:
  13.1 42.5 %all-reduce.19 = (bf16[1152]{0:T(1024)(128)(2,1)S(1)}, bf16[256]{0:T(256)(128)(2,1)S(1)}, bf16[256]{0:T(256)(128)(2,1)S(1)}, bf16[1152]{0:T(1024)(128)(2,1)S(1)}...) all-reduce(bf16[1152]{0:T(1024)(128)(2,1)S(1)} %dynamic-update-slic, ...), channel_id=1, replica_groups=mesh['seq'=4,'wide'=8] {'seq','wide'}, use_global_device_ids=true, to_apply=%add.4 | all-reduce | flops 5120 | bytes 20480
  55.6 70.0 %all-gather.1 = bf16[32,36,256]{2,1,0:T(8,128)(2,1)S(1)} all-gather(bf16[1,36,256]{2,1,0:T(8,128)(2,1)} %bitcast.221), channel_id=1, replica_groups=mesh['seq'=4,'wide'=8] {'seq','wide'}, dimensions={0}, use_global_device_ids=true | all-gather | bytes 608256 | tf_op jit(solution)/shard_map/all_gather | solution.py:81
  129.0 68.2 %all-gather.2 = bf16[32,36,256]{2,1,0:T(8,128)(2,1)S(1)} all-gather(bf16[1,36,256]{2,1,0:T(8,128)(2,1)S(1)} %bitcast.222), channel_id=1, replica_groups=mesh['seq'=4,'wide'=8] {'seq','wide'}, dimensions={0}, use_global_device_ids=true | all-gather | bytes 608256 | tf_op jit(solution)/shard_map/all_gather | solution.py:82
  218.4 34.6 %all-gather.15.cloned.1.call-done = bf16[2,2048,256]{2,1,0:T(8,128)(2,1)} async-done(((bf16[2,64,256]{2,1,0:T(8,128)(2,1)}), bf16[2,2048,256]{2,1,0:T(8,128)(2,1)}) %all-gather.15.cloned.1.call-update) | async-done | bytes 2097168 | tf_op jit(solution)/shard_map/all_gather | solution.py:140
  253.9 18.4 while.28
  282.3 30.0 %all-gather.17.cloned.1.call-done = bf16[1024,1152]{1,0:T(8,128)(2,1)} async-done(((bf16[32,1152]{1,0:T(8,128)(2,1)}), bf16[1024,1152]{1,0:T(8,128)(2,1)}) %all-gather.17.cloned.1.call-update) | async-done | bytes 2359312 | tf_op jit(solution)/shard_map/all_gather | solution.py:85
  315.3 118.0 %all-gather.23.cloned.1.call-done = bf16[32,36,6912]{2,1,0:T(8,128)(2,1)} async-done(((bf16[1,36,6912]{2,1,0:T(8,128)(2,1)}), bf16[32,36,6912]{2,1,0:T(8,128)(2,1)}) %all-gather.23.cloned.1.call-update) | async-done | bytes 15925264 | tf_op jit(solution)/shard_map/all_gather | solution.py:88
  433.3 18.5 reshape.382
  451.8 101.9 %all-gather.25.cloned.1.call-done = bf16[32,36,6912]{2,1,0:T(8,128)(2,1)} async-done(((bf16[1,36,6912]{2,1,0:T(8,128)(2,1)}), bf16[32,36,6912]{2,1,0:T(8,128)(2,1)}) %all-gather.25.cloned.1.call-update) | async-done | bytes 15925264 | tf_op jit(solution)/shard_map/all_gather | solution.py:89
  553.6 18.4 reshape.383
  588.1 77.6 %all-gather.19.cloned.1.call-done = bf16[6912,1152]{1,0:T(8,128)(2,1)} async-done(((bf16[216,1152]{1,0:T(8,128)(2,1)}), bf16[6912,1152]{1,0:T(8,128)(2,1)}) %all-gather.19.cloned.1.call-update) | async-done | bytes 15925264 | tf_op jit(solution)/shard_map/all_gather | solution.py:90
  686.4 11.7 fusion.104
  724.2 561.8 %while.29 = (s32[]{:T(128)}, bf16[2,256,256]{2,0,1:T(2,128)(2,1)}, f32[2,64,256]{2,1,0:T(8,128)}, bf16[2,64,256]{2,1,0:T(8,128)(2,1)}, bf16[2,256,256]{2,1,0:T(8...) while((s32[]{:T(128)}, bf16[2,256,256]{2,0,1:T(2,128)(2,1)}, ...), condition=%wide.region_17.18_spmd.clone, body=%wide.region_13.17_spmd.clone.sunk | while | flops 1348075264 | bytes 62660924 | solution.py:238
  743.5 124.6 %reduce-scatter.13.cloned.1.call-done = f32[64,256]{1,0:T(8,128)} async-done(((f32[2048,256]{1,0:T(8,128)}), f32[64,256]{1,0:T(8,128)}) %reduce-scatter.13.cloned.1.call-update) | async-done | bytes 65552 | tf_op jit(solution)/shard_map/while/body/eval_jaxpr/reduce_scatter | solution.py:229
  869.5 135.0 %reduce-scatter.11.cloned.1.call-done = f32[64,256]{1,0:T(8,128)} async-done(((f32[2048,256]{1,0:T(8,128)}), f32[64,256]{1,0:T(8,128)}) %reduce-scatter.11.cloned.1.call-update) | async-done | bytes 65552 | tf_op jit(solution)/shard_map/while/body/eval_jaxpr/reduce_scatter | solution.py:228
  1025.4 122.3 %reduce-scatter.13.cloned.1.call-done = f32[64,256]{1,0:T(8,128)} async-done(((f32[2048,256]{1,0:T(8,128)}), f32[64,256]{1,0:T(8,128)}) %reduce-scatter.13.cloned.1.call-update) | async-done | bytes 65552 | tf_op jit(solution)/shard_map/while/body/eval_jaxpr/reduce_scatter | solution.py:229
  1149.1 135.4 %reduce-scatter.11.cloned.1.call-done = f32[64,256]{1,0:T(8,128)} async-done(((f32[2048,256]{1,0:T(8,128)}), f32[64,256]{1,0:T(8,128)}) %reduce-scatter.11.cloned.1.call-update) | async-done | bytes 65552 | tf_op jit(solution)/shard_map/while/body/eval_jaxpr/reduce_scatter | solution.py:228
  1302.3 12.7 bitcast_dynamic-update-slice_fusion.3
  1315.0 12.6 bitcast_dynamic-update-slice_fusion.2
  1333.1 13.0 convolution_bitcast_fusion.1
  1349.7 39.2 %all-reduce.18 = (f32[1152]{0:T(1024)S(1)}, f32[256]{0:T(256)S(1)}, f32[256]{0:T(256)S(1)}, f32[1152]{0:T(1024)S(1)}, f32[1152]{0:T(1024)S(1)}, /*index=5*/f32[1152]{0:T(1024)S(1)}) all-reduce(f32[1152]{0:T(1024)S(1)} %get-tuple-element.160, f32[256]{0:T(256)S(1)} %get-tuple-element.156, ...), channel_id=4, replica_groups=mesh['seq'=4,'wide'=8] {'seq','wide'}, use_global_device_ids=true, to_apply=%region_22.23.clone | all-reduce | flops 5120 | bytes 40960
  1393.4 946.5 %all-reduce.22.cloned.1.call-done = f32[1152,15360]{1,0:T(8,128)} async-done(((f32[1152,15360]{1,0:T(8,128)}), f32[1152,15360]{1,0:T(8,128)}) %all-reduce.22.cloned.1.call-update) | async-done | bytes 70778896
  2347.0 105.9 %reduce-scatter.7.cloned.1.call-done = f32[32,1152]{1,0:T(8,128)} async-done(((f32[1024,1152]{1,0:T(8,128)}), f32[32,1152]{1,0:T(8,128)}) %reduce-scatter.7.cloned.1.call-update) | async-done | bytes 147472 | tf_op jit(solution)/shard_map/reduce_scatter | solution.py:270
  2452.9 319.7 %reduce-scatter.9.cloned.1.call-done = f32[216,1152]{1,0:T(8,128)} async-done(((f32[6912,1152]{1,0:T(8,128)}), f32[216,1152]{1,0:T(8,128)}) %reduce-scatter.9.cloned.1.call-update) | async-done | bytes 995344
  (336 shorter events, 205.6 us)
Async XLA Ops:
  7.2 193.7 %all-gather.21.cloned.1.call-start = ((), (), s32[]{:S(2)}) async-start(), calls=%async_computation.13 | async-start | bytes 2703360 | tf_op jit(solution)/shard_map/all_gather | solution.py:80
  7.9 210.5 %all-gather.13.cloned.1.call-start = ((), (), s32[]{:S(2)}) async-start(), calls=%async_computation.8 | async-start | bytes 2162688 | tf_op jit(solution)/shard_map/all_gather | solution.py:139
  129.0 124.1 %all-gather.15.cloned.1.call-start = ((), (), s32[]{:S(2)}) async-start(), calls=%async_computation.9 | async-start | bytes 2162688 | tf_op jit(solution)/shard_map/all_gather | solution.py:140
  198.3 113.9 %all-gather.17.cloned.1.call-start = ((), (), s32[]{:S(2)}) async-start(), calls=%async_computation.10 | async-start | bytes 2433024 | tf_op jit(solution)/shard_map/all_gather | solution.py:85
  198.9 234.4 %all-gather.23.cloned.1.call-start = ((), (), s32[]{:S(2)}) async-start(), calls=%async_computation.14 | async-start | bytes 18247680 | tf_op jit(solution)/shard_map/all_gather | solution.py:88
  199.5 354.1 %all-gather.25.cloned.1.call-start = ((), (), s32[]{:S(2)}) async-start(), calls=%async_computation.15 | async-start | bytes 18247680 | tf_op jit(solution)/shard_map/all_gather | solution.py:89
  200.1 465.6 %all-gather.19.cloned.1.call-start = ((), (), s32[]{:S(2)}) async-start(), calls=%async_computation.11 | async-start | bytes 16422912 | tf_op jit(solution)/shard_map/all_gather | solution.py:90
  208.3 9.4 all-to-all-start
  272.3 9.6 all-to-all-start.1
  315.2 265.0 %copy-start.18 = (bf16[2,64,1152]{2,1,0:T(8,128)(2,1)}, bf16[2,64,1152]{2,1,0:T(8,128)(2,1)S(1)}, u32[]{:S(2)}) copy-start(bf16[2,64,1152]{2,1,0:T(8,128)(2,1)S(1)} %multiply_convert_fusion.3) | copy-start | bytes 884740
  713.1 9.4 all-to-all-start.2
  724.1 565.7 %copy-start.35 = (f32[64,128]{1,0:T(8,128)S(1)}, f32[64,128]{1,0:T(8,128)}, u32[]{:S(2)}) copy-start(f32[64,128]{1,0:T(8,128)} %copy-done.34) | copy-start | bytes 98308
  724.1 565.7 %copy-start.37 = (f32[64,128]{1,0:T(8,128)S(1)}, f32[64,128]{1,0:T(8,128)}, u32[]{:S(2)}) copy-start(f32[64,128]{1,0:T(8,128)} %copy-done.36) | copy-start | bytes 98308
  724.1 566.6 %copy-start.58 = (f32[2,64]{1,0:T(2,128)S(1)}, f32[2,64]{1,0:T(2,128)}, u32[]{:S(2)}) copy-start(f32[2,64]{1,0:T(2,128)} %copy-done.57) | copy-start | bytes 1540
  724.1 566.6 %copy-start.66 = (f32[256]{0:T(256)S(1)}, f32[256]{0:T(256)}, u32[]{:S(2)}) copy-start(f32[256]{0:T(256)} %copy-done.65) | copy-start | bytes 3076
  724.2 567.7 %copy-start.76 = (f32[2,64]{1,0:T(2,128)S(1)}, f32[2,64]{1,0:T(2,128)}, u32[]{:S(2)}) copy-start(f32[2,64]{1,0:T(2,128)} %copy-done.75) | copy-start | bytes 1540
  724.2 143.9 %reduce-scatter.13.cloned.1.call-start = ((), (), s32[]{:S(2)}) async-start(), calls=%async_computation.19 | async-start | bytes 2162688 | tf_op jit(solution)/shard_map/while/body/eval_jaxpr/reduce_scatter | solution.py:229
  732.2 272.4 %reduce-scatter.11.cloned.1.call-start = ((), (), s32[]{:S(2)}) async-start(), calls=%async_computation.18 | async-start | bytes 2162688 | tf_op jit(solution)/shard_map/while/body/eval_jaxpr/reduce_scatter | solution.py:228
  1006.1 141.6 %reduce-scatter.13.cloned.1.call-start = ((), (), s32[]{:S(2)}) async-start(), calls=%async_computation.19 | async-start | bytes 2162688 | tf_op jit(solution)/shard_map/while/body/eval_jaxpr/reduce_scatter | solution.py:229
  1014.0 270.5 %reduce-scatter.11.cloned.1.call-start = ((), (), s32[]{:S(2)}) async-start(), calls=%async_computation.18 | async-start | bytes 2162688 | tf_op jit(solution)/shard_map/while/body/eval_jaxpr/reduce_scatter | solution.py:228
  1286.0 9.6 all-to-all-start.3
  1289.5 1050.4 %all-reduce.22.cloned.1.call-start = ((), (), s32[]{:S(2)}) async-start(), calls=%async_computation.16 | async-start | bytes 141557760
  1327.6 1125.2 %reduce-scatter.7.cloned.1.call-start = ((), (), s32[]{:S(2)}) async-start(), calls=%async_computation.12 | async-start | bytes 4866048 | tf_op jit(solution)/shard_map/reduce_scatter | solution.py:270
  1331.6 1440.9 %reduce-scatter.9.cloned.1.call-start = ((), (), s32[]{:S(2)}) async-start(), calls=%async_computation.17 | async-start | bytes 32845824
  (75 other events, 1632.8 us)
Sparse Core Ops, SparseCore 0:
  10.9 62.1 all-gather.20
  129.1 55.4 all-gather.12
  198.4 54.5 all-gather.14
  255.9 56.3 all-gather.16
  315.1 118.1 all-gather.22
  436.1 117.4 all-gather.24
  556.5 109.1 all-gather.18
  732.3 135.7 reduce-scatter.12
  870.5 134.0 reduce-scatter.10
  1014.1 133.4 reduce-scatter.12
  1150.0 134.4 reduce-scatter.10
  1327.7 1012.1 all-reduce.21
  2346.0 106.7 reduce-scatter.6
  2460.8 311.6 reduce-scatter.8
where the time goes:
time: 2790 us; the launch traced here: 2780 us
  waiting for transfers between devices  2270 us (81%)
  blocking collectives  220 us (8%)
  matrix products  133 us (5%)
  local copies, waits for them, and re-layouts  104 us (4%)
    unnamed x12, waiting for transfers between devices  1270 us
    reduce_scatter x2, waiting for transfers between devices, backward_tail(): lax.psum_scatter(grad_keys, ('seq', 'wide'), scatter_dimension=0, tiled=T...  270 us
    reduce_scatter x2, waiting for transfers between devices, backward_tail(): lax.psum_scatter(grad_values, ('seq', 'wide'), scatter_dimension=0, tiled...  247 us
    all_gather x1, waiting for transfers between devices, on_device(): lax.all_gather(w_gate, ('seq', 'wide'), axis=0, tiled=True)  118 us
    reduce_scatter x1, waiting for transfers between devices, on_device(): lax.psum_scatter(row_product(token_heads, d_branch), ('seq', 'wide'), sca...  106 us
    all_gather x1, waiting for transfers between devices, on_device(): lax.all_gather(w_up, ('seq', 'wide'), axis=0, tiled=True)  102 us
    unnamed x2, blocking collectives  81.7 us
    all_gather x1, waiting for transfers between devices, on_device(): lax.all_gather(w_down, ('seq', 'wide'), axis=0, tiled=True)  77.6 us
  transfers between devices with their start and end apart: 18, of which 16 were waited for; matrix products, arithmetic and copies ran while one was open for 5% of the time, Pallas kernels for 0%

commit v1 on v0

v1 whole, which is shorter than its diff:
```python
import jax
import jax.numpy as jnp
from jax import lax
from jax.sharding import Mesh
from jax.sharding import PartitionSpec as P

EPSILON = 1e-06
ROPE_BASE = 1000000.0
SCORE_SCALE = 0.0625
MASKED = -1e30


def root_norm(values, gain_vector):
    return (
        values
        * lax.rsqrt(jnp.mean(values * values, axis=-1, keepdims=True) + EPSILON)
        * gain_vector
    )


def rotation(positions, width):
    half_width = width // 2
    frequency = ROPE_BASE ** (-2.0 * jnp.arange(half_width).astype(jnp.float32) / width)
    angles = positions.astype(jnp.float32)[:, None] * frequency[None, :]
    return (jnp.cos(angles), jnp.sin(angles))


def rotate(values, cosine, sine_table):
    half_width = values.shape[-1] // 2
    first_half = values[..., :half_width]
    second_half = values[..., half_width:]
    return jnp.concatenate(
        [
            first_half * cosine - second_half * sine_table,
            second_half * cosine + first_half * sine_table,
        ],
        axis=-1,
    )


def flat_norm_pull(values, gain_vector):
    return jax.vjp(root_norm, values, gain_vector)


def spread_sum(parts, axes):
    moved = lax.all_to_all(
        parts.astype(jnp.bfloat16), axes, split_axis=0, concat_axis=0, tiled=True
    )
    return jnp.sum(moved.astype(jnp.float32), axis=0)


def on_device(
    tokens,
    out_grad,
    norm_attn,
    w_query,
    w_key,
    w_value,
    norm_query,
    norm_key,
    w_output,
    norm_attn_post,
    norm_ffw,
    w_gate,
    w_up,
    w_down,
    norm_ffw_post,
):
    low = jnp.bfloat16
    full = jnp.float32
    seqs, rows, width = tokens.shape
    S = lax.axis_size("seq")
    Z = lax.axis_size("wz")
    X = lax.axis_size("wx")
    everyone = ("seq", "wz", "wx")
    group = ("seq", "wx")
    count = S * Z * X
    ranks = S * X
    heads = S
    head_dim = w_key.shape[1]
    qwidth = heads * head_dim
    wrows = w_query.shape[0]
    orows = w_output.shape[0]
    units = w_down.shape[0]
    mine = count // ranks * units
    padded = -(-mine // 128) * 128
    own = seqs * rows

    def dot(left, right):
        return jnp.dot(left, right, preferred_element_type=full)

    def dot_t(left, right):
        return jnp.einsum("nc,dc->nd", left, right, preferred_element_type=full)

    def t_dot(left, right):
        return jnp.einsum("nd,nc->dc", left, right, preferred_element_type=full)

    def column(vector):
        return jnp.pad(vector, (0, wrows - vector.shape[0]))[:, None]

    gains_own = jnp.concatenate(
        [
            column(v)
            for v in (norm_attn, norm_attn_post, norm_ffw, norm_ffw_post, norm_query, norm_key)
        ],
        axis=1,
    )
    gains_own = jnp.pad(gains_own, ((0, 0), (0, 128 - gains_own.shape[1])))
    qkv_width = qwidth + 2 * head_dim
    pack = jnp.concatenate(
        [w_query, w_key, w_value, gains_own, w_output.reshape(wrows, qwidth)], axis=1
    )
    packed = lax.all_gather(pack, everyone, axis=0, tiled=False)
    qkv_weight = packed[:, :, :qkv_width].reshape(width, qkv_width)
    output_weight = packed[:, :, qkv_width + 128 :].reshape(qwidth, width)
    gain_block = packed[:, :, qkv_width : qkv_width + 8].astype(full)
    gain_attn, gain_attn_post, gain_ffw, gain_ffw_post = (
        gain_block[:, :, i].reshape(width) for i in range(4)
    )
    gain_query, gain_key = (
        gain_block[:, : norm_query.shape[0], i].reshape(head_dim) for i in (4, 5)
    )

    def by_rank(weight):
        cut = weight.reshape(wrows, S, Z, X, units).transpose(1, 3, 0, 2, 4)
        return jnp.pad(cut.reshape(ranks, wrows, mine), ((0, 0), (0, 0), (0, padded - mine)))

    sent = jnp.concatenate([by_rank(w_gate), by_rank(w_up)], axis=2)
    arrived = lax.all_to_all(sent, group, split_axis=0, concat_axis=0, tiled=True)
    hidden_weight = lax.all_gather(
        arrived.reshape(ranks * wrows, 2 * padded), "wz", axis=0, tiled=True
    )
    down_weight = lax.all_gather(w_down, "wz", axis=0, tiled=True)

    place = jnp.arange(width, dtype=jnp.int32)
    block = place // wrows
    natural = (
        ((block // X % S) * Z + block // (S * X)) * X + block % X
    ) * wrows + place % wrows
    shuffle = (place[:, None] == natural[None, :]).astype(low)

    block_index = lax.axis_index(everyone)
    local_pos = block_index * rows + jnp.arange(rows, dtype=jnp.int32)
    cosine, sine_table = rotation(local_pos, head_dim)
    cosine = jnp.tile(cosine, (seqs, 1))
    sine_table = jnp.tile(sine_table, (seqs, 1))

    def query_side(raw_values, gain_vector):
        return rotate(
            root_norm(raw_values, gain_vector), cosine[:, None, :], sine_table[:, None, :]
        )

    def key_side(raw_values, gain_vector):
        return rotate(root_norm(raw_values, gain_vector), cosine, sine_table)

    layer_in = tokens.reshape(own, width).astype(full)
    upstream = out_grad.reshape(own, width).astype(full)
    normed_f, attn_in_pull = flat_norm_pull(layer_in, gain_attn)
    normed = normed_f.astype(low)
    qkv_raw = dot(normed, qkv_weight)
    query_raw = qkv_raw[:, :qwidth].reshape(own, heads, head_dim)
    key_raw = qkv_raw[:, qwidth : qwidth + head_dim]
    value_raw = qkv_raw[:, qwidth + head_dim :]
    key_shaped, key_pull = jax.vjp(key_side, key_raw, gain_key)
    kv_own = jnp.concatenate([key_shaped, value_raw], axis=1).astype(low)
    all_kv = lax.all_gather(
        kv_own.reshape(seqs, rows, 2 * head_dim), everyone, axis=1, tiled=True
    )
    query_shaped, query_pull = jax.vjp(query_side, query_raw, gain_query)
    queries = query_shaped.astype(low).reshape(seqs, rows * heads, head_dim)
    all_keys = all_kv[:, :, :head_dim]
    all_values = all_kv[:, :, head_dim:]
    total_len = all_kv.shape[1]
    query_pos = block_index * rows + jnp.arange(rows * heads, dtype=jnp.int32) // heads
    allowed = jnp.arange(total_len, dtype=jnp.int32)[None, :] <= query_pos[:, None]

    scores = (
        jnp.einsum("bqd,bkd->bqk", queries, all_keys, preferred_element_type=full) * SCORE_SCALE
    )
    scores = jnp.where(allowed[None], scores, MASKED)
    peak = jnp.max(scores, axis=-1, keepdims=True)
    exponent = jnp.exp(scores - peak)
    total = jnp.sum(exponent, axis=-1, keepdims=True)
    probs_f = exponent / total
    probs = probs_f.astype(low)
    attended = jnp.einsum("bqk,bkd->bqd", probs, all_values, preferred_element_type=full)
    token_heads = attended.astype(low).reshape(own, qwidth)
    branch = dot(token_heads, output_weight)
    branch_normed, attn_post_pull = flat_norm_pull(branch, gain_attn_post)
    mixed = layer_in + branch_normed
    normed_ffw_f, ffw_in_pull = flat_norm_pull(mixed, gain_ffw)
    normed_ffw = dot(normed_ffw_f.astype(low), shuffle).astype(low)

    normed_all = lax.all_gather(normed_ffw, group, axis=0, tiled=True)
    hidden = dot(normed_all, hidden_weight)
    gate = hidden[:, :padded]
    upward = hidden[:, padded:]
    middle_f, middle_pull = jax.vjp(gelu_gate, gate, upward)
    middle = middle_f.astype(low)[:, :mine]
    output_raw = spread_sum(dot(middle, down_weight).reshape(ranks, own, width), group)
    output_normed, ffw_post_pull = flat_norm_pull(output_raw, gain_ffw_post)
    layer_out = (mixed + output_normed).astype(low).reshape(tokens.shape)

    d_output_f, grad_ffw_post = ffw_post_pull(upstream)
    d_output = lax.all_gather(d_output_f.astype(low), group, axis=0, tiled=True)
    d_middle = jnp.pad(dot_t(d_output, down_weight), ((0, 0), (0, padded - mine)))
    d_gate, d_up = middle_pull(d_middle)
    d_hidden = jnp.concatenate([d_gate.astype(low), d_up.astype(low)], axis=1)
    d_shuffled = spread_sum(dot_t(d_hidden, hidden_weight).reshape(ranks, own, width), group)
    grad_down = lax.psum_scatter(
        t_dot(middle, d_output).astype(low), "wz", scatter_dimension=0, tiled=True
    ).astype(full)
    grad_hidden = lax.psum_scatter(
        t_dot(normed_all, d_hidden).astype(low), "wz", scatter_dimension=0, tiled=True
    )
    coarse = d_shuffled.astype(low)
    fine = (d_shuffled - coarse.astype(full)).astype(low)
    d_normed_ffw = dot_t(coarse, shuffle) + dot_t(fine, shuffle)
    d_mixed_part, grad_ffw = ffw_in_pull(d_normed_ffw)
    d_mixed = upstream + d_mixed_part
    d_branch_f, grad_attn_post = attn_post_pull(d_mixed)
    d_branch = d_branch_f.astype(low)
    d_attended = dot_t(d_branch, output_weight).astype(low)
    d_attended = d_attended.reshape(seqs, rows * heads, head_dim)

    d_probs = jnp.einsum("bqd,bkd->bqk", d_attended, all_values, preferred_element_type=full)
    centre = jnp.sum(probs_f * d_probs, axis=-1, keepdims=True)
    d_scores = (probs_f * (d_probs - centre)).astype(low)
    part_values = jnp.einsum("bqk,bqd->bkd", probs, d_attended, preferred_element_type=full)
    part_keys = (
        jnp.einsum("bqk,bqd->bkd", d_scores, queries, preferred_element_type=full) * SCORE_SCALE
    )
    part_kv = jnp.concatenate([part_keys.astype(low), part_values.astype(low)], axis=2)
    part_kv = part_kv.reshape(seqs, S, Z, X, rows, 2 * head_dim).transpose(1, 3, 2, 0, 4, 5)
    part_kv = spread_sum(part_kv.reshape(ranks, Z * own, 2 * head_dim), group)
    d_kv = spread_sum(part_kv.reshape(Z, own, 2 * head_dim), "wz")
    d_queries = (
        jnp.einsum("bqk,bkd->bqd", d_scores, all_keys, preferred_element_type=full) * SCORE_SCALE
    )
    d_query_raw_f, grad_query_gain = query_pull(d_queries.reshape(own, heads, head_dim))
    d_key_raw_f, grad_key_gain = key_pull(d_kv[:, :head_dim])
    d_qkv = jnp.concatenate(
        [
            d_query_raw_f.reshape(own, qwidth).astype(low),
            d_key_raw_f.astype(low),
            d_kv[:, head_dim:].astype(low),
        ],
        axis=1,
    )
    d_input_part, grad_attn = attn_in_pull(dot_t(d_qkv, qkv_weight))
    input_grad = (d_mixed + d_input_part).reshape(tokens.shape)

    def scatter(matrix, block_rows):
        columns = matrix.size // (count * block_rows)
        blocks = matrix.astype(low).reshape(S, Z, X, block_rows, columns).transpose(0, 2, 1, 3, 4)
        part = spread_sum(blocks.reshape(ranks, Z * block_rows, columns), group)
        return spread_sum(part.reshape(Z, block_rows, columns), "wz")

    out_blocks = t_dot(token_heads, d_branch).astype(low).reshape(S, Z, X, orows, width)
    out_blocks = out_blocks.transpose(0, 2, 1, 3, 4).reshape(qwidth, width)
    out_part = lax.psum_scatter(out_blocks, group, scatter_dimension=0, tiled=True)
    grad_output = lax.psum_scatter(out_part, "wz", scatter_dimension=0, tiled=True).astype(full)

    grad_qkv = scatter(t_dot(normed, d_qkv), wrows)
    grad_query_w = grad_qkv[:, :qwidth]
    grad_key_w = grad_qkv[:, qwidth : qwidth + head_dim]
    grad_value_w = grad_qkv[:, qwidth + head_dim :]

    returned = lax.all_to_all(
        grad_hidden.reshape(ranks, wrows, 2 * padded), group, split_axis=0, concat_axis=0, tiled=True
    )

    def natural_columns(part):
        cut = part[:, :, :mine].reshape(S, X, wrows, Z, units).transpose(2, 0, 3, 1, 4)
        return cut.reshape(wrows, count * units).astype(full)

    grad_gate = natural_columns(returned[:, :, :padded])
    grad_upward = natural_columns(returned[:, :, padded:])

    gain_grads = [
        grad_attn,
        grad_query_gain,
        grad_key_gain,
        grad_attn_post,
        grad_ffw,
        grad_ffw_post,
    ]
    gain_rows = jnp.concatenate([g.reshape(count, -1) for g in gain_grads], axis=1)
    gain_sums = jnp.sum(
        lax.all_to_all(gain_rows, everyone, split_axis=0, concat_axis=0, tiled=True), axis=0
    )
    gains = []
    start = 0
    for g in gain_grads:
        size = g.size // count
        gains.append(gain_sums[start : start + size])
        start += size
    return (
        layer_out,
        input_grad,
        gains[0],
        grad_query_w,
        grad_key_w,
        grad_value_w,
        gains[1],
        gains[2],
        grad_output,
        gains[3],
        gains[4],
        grad_gate,
        grad_upward,
        grad_down,
        gains[5],
    )


def gelu_gate(gate_in, up_in):
    return jax.nn.gelu(gate_in, approximate=True) * up_in


def solution(mesh):
    seq_size, wide_size = mesh.devices.shape
    mesh = Mesh(
        mesh.devices.reshape(seq_size, wide_size // 2, 2), ("seq", "wz", "wx")
    )
    placed = (
        P(None, ("seq", "wz", "wx"), None),
        P(None, ("seq", "wz", "wx"), None),
        P(("seq", "wz", "wx")),
        P(("seq", "wz", "wx"), None),
        P(("seq", "wz", "wx"), None),
        P(("seq", "wz", "wx"), None),
        P(("seq", "wz", "wx")),
        P(("seq", "wz", "wx")),
        P(("seq", "wz", "wx"), None),
        P(("seq", "wz", "wx")),
        P(("seq", "wz", "wx")),
        P(("seq", "wz", "wx"), None),
        P(("seq", "wz", "wx"), None),
        P(("seq", "wz", "wx"), None),
        P(("seq", "wz", "wx")),
    )
    return jax.shard_map(
        on_device,
        mesh=mesh,
        in_specs=placed,
        out_specs=(
            P(None, ("seq", "wz", "wx"), None),
            P(None, ("seq", "wz", "wx"), None),
            P(("seq", "wz", "wx")),
            P(("seq", "wz", "wx"), None),
            P(("seq", "wz", "wx"), None),
            P(("seq", "wz", "wx"), None),
            P(("seq", "wz", "wx")),
            P(("seq", "wz", "wx")),
            P(("seq", "wz", "wx"), None),
            P(("seq", "wz", "wx")),
            P(("seq", "wz", "wx")),
            P(("seq", "wz", "wx"), None),
            P(("seq", "wz", "wx"), None),
            P(("seq", "wz", "wx"), None),
            P(("seq", "wz", "wx")),
        ),
        check_vma=False,
    )
```

time: 2790 us -> 709 us (0.25)
  waiting for transfers between devices: 2270 us -> 365 us
  blocking collectives: 220 us -> 53.9 us
  matrix products: 133 us -> 71 us
  other arithmetic: 16.8 us -> 57.6 us
    unnamed x12 -> x11, waiting for transfers between devices: 1270 us -> 0.53 us
    reduce_scatter x5 -> x3, waiting for transfers between devices: 623 us -> 56 us  [the longest x1 43.3 us: on_device(): lax.psum_scatter(t_dot(normed_all, d_hidden).astype(low), 'wz', scatter_d...]
    all_gather x2 -> x0, blocking collectives: 138 us -> none  [the longest x1 70 us: on_device(): lax.all_gather(w_key, ('seq', 'wide'), axis=0, tiled=True)]
    all_gather x7 -> x6, waiting for transfers between devices: 362 us -> 240 us  [the longest x1 72.2 us: on_device(): packed = lax.all_gather(pack, everyone, axis=0, tiled=False)]
    unnamed x2 -> x0, blocking collectives: 81.7 us -> none
    dot_general x35 -> x20, matrix products: 133 us -> 65.7 us  [the longest x4 18.3 us: t_dot(): return jnp.einsum('nd,nc->dc', left, right, preferred_element_type=full)]
    all_to_all x0 -> x2, blocking collectives: none -> 53.9 us  [the longest x1 31.5 us: spread_sum(): lax.all_to_all(parts.astype(jnp.bfloat16), axes, split_axis=0, concat_axi...]
    all_to_all x4 -> x7, waiting for transfers between devices: 20 us -> 68.5 us  [the longest x5 60.1 us: spread_sum(): lax.all_to_all(parts.astype(jnp.bfloat16), axes, split_axis=0, concat_axi...]
  transfers between devices with their start and end apart: 18 -> 17, of which waited for: 16 -> 13; matrix products, arithmetic and copies ran while one was open for 5% -> 23% of each run, Pallas kernels for 0% -> 0%
where the time goes in v1:
time: 709 us; the launch traced here: 700 us
  waiting for transfers between devices  365 us (51%)
  local copies, waits for them, and re-layouts  106 us (15%)
  matrix products  71 us (10%)
  other arithmetic  57.6 us (8%)
  blocking collectives  53.9 us (8%)
  starting transfers between devices  31.4 us (4%)
  between operations  15.4 us (2%)
    all_gather x1, waiting for transfers between devices, on_device(): packed = lax.all_gather(pack, everyone, axis=0, tiled=False)  72.2 us
    all_gather x1, waiting for transfers between devices, on_device(): lax.all_gather(arrived.reshape(ranks * wrows, 2 * padded), 'wz', axis=0,...  64.4 us
    all_to_all x5, waiting for transfers between devices, spread_sum(): lax.all_to_all(parts.astype(jnp.bfloat16), axes, split_axis=0, concat_axi...  60.1 us
    reduce_scatter x1, waiting for transfers between devices, on_device(): lax.psum_scatter(t_dot(normed_all, d_hidden).astype(low), 'wz', scatter_d...  43.3 us
    all_gather x1, waiting for transfers between devices, on_device(): down_weight = lax.all_gather(w_down, 'wz', axis=0, tiled=True)  33.1 us
    all_to_all x1, blocking collectives, spread_sum(): lax.all_to_all(parts.astype(jnp.bfloat16), axes, split_axis=0, concat_axi...  31.5 us
    all_gather x1, waiting for transfers between devices, on_device(): normed_all = lax.all_gather(normed_ffw, group, axis=0, tiled=True)  29.9 us
    all_gather x1, waiting for transfers between devices, on_device(): d_output = lax.all_gather(d_output_f.astype(low), group, axis=0, tiled=True)  26.5 us
  transfers between devices with their start and end apart: 17, of which 13 were waited for; matrix products, arithmetic and copies ran while one was open for 23% of the time, Pallas kernels for 0%

profile of v1, /device:TPU:0, one launch (start us, length us, event | category | flops | bytes accessed | tf_op | source)
XLA Modules:
  0.0 700.1 jit_solution(1865673613000954246)
XLA Ops:
  15.4 72.2 %all-gather.19.cloned.1.call-done = bf16[32,36,2688]{2,1,0:T(8,128)(2,1)} async-done(((bf16[1,36,2688]{2,1,0:T(8,128)(2,1)}), bf16[32,36,2688]{2,1,0:T(8,128)(2,1)}) %all-gather.19.cloned.1.call-update) | async-done | bytes 6193168 | tf_op jit(solution)/shard_map/all_gather | solution.py:113
  119.6 22.4 %all_to_all.49 = bf16[8,36,1792]{2,1,0:T(8,128)(2,1)S(1)} all-to-all(bf16[8,36,1792]{2,1,0:T(8,128)(2,1)S(1)} %copy.119), channel_id=1, replica_groups=mesh['seq'=4,'wz'=4,'wx'=2] {'seq','wx'}, dimensions={0} | all-to-all | bytes 2064384 | tf_op jit(solution)/shard_map/all_to_all | solution.py:129
  156.5 14.1 %all-gather.9.cloned.1.call-done = bf16[2,2048,512]{2,1,0:T(8,128)(2,1)} async-done(((bf16[2,64,512]{2,1,0:T(8,128)(2,1)}), bf16[2,2048,512]{2,1,0:T(8,128)(2,1)}) %all-gather.9.cloned.1.call-update) | async-done | bytes 4194320 | tf_op jit(solution)/shard_map/all_gather | solution.py:166
  170.6 5.3 fusion.114
  186.6 64.4 %all-gather.13.cloned.1.call-done = bf16[1152,1792]{1,0:T(8,128)(2,1)} async-done(((bf16[288,1792]{1,0:T(8,128)(2,1)}), bf16[1152,1792]{1,0:T(8,128)(2,1)}) %all-gather.13.cloned.1.call-update) | async-done | bytes 4128784 | tf_op jit(solution)/shard_map/all_gather | solution.py:130
  251.0 29.9 %all-gather.11.cloned.1.call-done = bf16[1024,1152]{1,0:T(8,128)(2,1)} async-done(((bf16[128,1152]{1,0:T(8,128)(2,1)}), bf16[1024,1152]{1,0:T(8,128)(2,1)}) %all-gather.11.cloned.1.call-update) | async-done | bytes 2359312 | tf_op jit(solution)/shard_map/all_gather | solution.py:194
  280.9 7.8 %fusion.118 = f32[1024,1792]{1,0:T(8,128)S(1)} fusion(bf16[1024,1152]{1,0:T(8,128)(2,1)} %all-gather.11.cloned.1.call-done, bf16[1152,1792]{1,0:T(8,128)(2,1)} %all-gather.13.cloned.1.call-done), kind=kOutput, calls=%fused_computation.239 | convolution fusion | flops 4227858432 | bytes 13828096 | tf_op jit(solution)/shard_map/dot_general | solution.py:90
  293.3 33.1 %all-gather.15.cloned.1.call-done = bf16[864,1152]{1,0:T(8,128)(2,1)} async-done(((bf16[216,1152]{1,0:T(8,128)(2,1)}), bf16[864,1152]{1,0:T(8,128)(2,1)}) %all-gather.15.cloned.1.call-update) | async-done | bytes 1990672 | tf_op jit(solution)/shard_map/all_gather | solution.py:133
  326.4 6.5 convolution_convert_fusion.4
  338.1 28.2 %all-to-all-done.1 = bf16[8,128,1152]{2,1,0:T(8,128)(2,1)} async-done(((bf16[8,128,1152]{2,1,0:T(8,128)(2,1)}), bf16[8,128,1152]{2,1,0:T(8,128)(2,1)}, u32[]{:S(2)}, u32[]{:S(2)}) %all-to-all-start.1) | async-done | bytes 2359328 | tf_op jit(solution)/shard_map/all_to_all | solution.py:46
  377.1 26.5 %all-gather.17.cloned.1.call-done = bf16[1024,1152]{1,0:T(8,128)(2,1)} async-done(((bf16[128,1152]{1,0:T(8,128)(2,1)}), bf16[1024,1152]{1,0:T(8,128)(2,1)}) %all-gather.17.cloned.1.call-update) | async-done | bytes 2359312 | tf_op jit(solution)/shard_map/all_gather | solution.py:205
  403.6 5.1 fusion.119
  408.7 5.1 fusion.11
  413.8 5.2 convolution_convert_fusion.3
  419.0 31.5 %all_to_all.50 = bf16[8,128,1152]{2,1,0:T(8,128)(2,1)S(1)} all-to-all(bf16[8,128,1152]{2,1,0:T(8,128)(2,1)S(1)} %bitcast.131), channel_id=1, replica_groups=mesh['seq'=4,'wz'=4,'wx'=2] {'seq','wx'}, dimensions={0} | all-to-all | bytes 4718592 | tf_op jit(solution)/shard_map/all_to_all | solution.py:46
  458.8 6.1 convolution_convert_fusion.5
  475.8 6.3 copy.125
  491.3 12.8 %reduce-scatter.7.cloned.1.call-done = bf16[128,1152]{1,0:T(8,128)(2,1)} async-done(((bf16[1024,1152]{1,0:T(8,128)(2,1)}), bf16[128,1152]{1,0:T(8,128)(2,1)}) %reduce-scatter.7.cloned.1.call-update) | async-done | bytes 294928 | tf_op jit(solution)/shard_map/reduce_scatter | solution.py:261
  504.6 9.2 %convolution_convert_fusion = bf16[1152,1792]{1,0:T(8,128)(2,1)} fusion(bf16[1024,1152]{1,0:T(8,128)(2,1)} %all-gather.11.cloned.1.call-done, bf16[1024,896]{1,0:T(8,128)(2,1)} %copy-done.17, bf16[1024,896]{1,0:T(8,128)(2,1)} %copy-done.16), kind=kOutput, calls=%fused_computation.1 | convolution fusion | flops 4237262848 | bytes 10158080 | tf_op jit(solution)/shard_map/nd,nc->dc/dot_general | solution.py:96
  520.4 22.6 %all-to-all-done.3 = bf16[8,512,512]{2,1,0:T(8,128)(2,1)} async-done(((bf16[8,512,512]{2,1,0:T(8,128)(2,1)}), bf16[8,512,512]{2,1,0:T(8,128)(2,1)}, u32[]{:S(2)}, u32[]{:S(2)}) %all-to-all-start.3) | async-done | bytes 4194336 | tf_op jit(solution)/shard_map/all_to_all | solution.py:46
  563.7 5.5 all-to-all-done.4
  594.3 5.7 reshape.536
  608.1 43.3 %reduce-scatter.11.cloned.1.call-done = bf16[288,1792]{1,0:T(8,128)(2,1)} async-done(((bf16[1152,1792]{1,0:T(8,128)(2,1)}), bf16[288,1792]{1,0:T(8,128)(2,1)}) %reduce-scatter.11.cloned.1.call-update) | async-done | bytes 1032208 | tf_op jit(solution)/shard_map/reduce_scatter | solution.py:213
  665.6 8.4 %all-to-all-done.8 = bf16[8,36,1792]{2,1,0:T(8,128)(2,1)} async-done(((bf16[8,36,1792]{2,1,0:T(8,128)(2,1)}), bf16[8,36,1792]{2,1,0:T(8,128)(2,1)}, u32[]{:S(2)}, u32[]{:S(2)}) %all-to-all-start.8) | async-done | bytes 1032224 | tf_op jit(solution)/shard_map/all_to_all | solution.py:269
  (304 shorter events, 207.8 us)
Async XLA Ops:
  7.2 80.5 %all-gather.19.cloned.1.call-start = ((), (), s32[]{:S(2)}) async-start(), calls=%async_computation.21 | async-start | bytes 7096320 | tf_op jit(solution)/shard_map/all_gather | solution.py:113
  12.8 157.8 %all-gather.9.cloned.1.call-start = ((), (), s32[]{:S(2)}) async-start(), calls=%async_computation.13 | async-start | bytes 4325376 | tf_op jit(solution)/shard_map/all_gather | solution.py:166
  108.0 143.1 %all-gather.13.cloned.1.call-start = ((), (), s32[]{:S(2)}) async-start(), calls=%async_computation.15 | async-start | bytes 5160960 | tf_op jit(solution)/shard_map/all_gather | solution.py:130
  119.6 25.9 %copy-start.34 = (f32[32,8]{1,0:T(8,128)S(1)}, f32[32,8]{1,0:T(8,128)}, u32[]{:S(2)}) copy-start(f32[32,8]{1,0:T(8,128)} %get-tuple-element.29) | copy-start | bytes 3076
  119.6 26.0 %copy-start.33 = (f32[32,36]{1,0:T(8,128)S(1)}, f32[32,36]{1,0:T(8,128)}, u32[]{:S(2)}) copy-start(f32[32,36]{1,0:T(8,128)} %get-tuple-element.26) | copy-start | bytes 13828
  119.6 26.7 %copy-start.32 = (f32[32,36]{1,0:T(8,128)S(1)}, f32[32,36]{1,0:T(8,128)}, u32[]{:S(2)}) copy-start(f32[32,36]{1,0:T(8,128)} %get-tuple-element.27) | copy-start | bytes 13828
  143.1 137.8 %all-gather.11.cloned.1.call-start = ((), (), s32[]{:S(2)}) async-start(), calls=%async_computation.14 | async-start | bytes 2654208 | tf_op jit(solution)/shard_map/all_gather | solution.py:194
  183.0 105.7 %copy-start.5 = (f32[128,1152]{1,0:T(8,128)}, f32[128,1152]{1,0:T(8,128)S(1)}, u32[]{:S(2)}) copy-start(f32[128,1152]{1,0:T(8,128)S(1)} %get-tuple-element.35) | copy-start | bytes 1769476
  186.0 140.3 %all-gather.15.cloned.1.call-start = ((), (), s32[]{:S(2)}) async-start(), calls=%async_computation.16 | async-start | bytes 2488320 | tf_op jit(solution)/shard_map/all_gather | solution.py:133
  332.8 33.5 %all-to-all-start.1 = ((bf16[8,128,1152]{2,1,0:T(8,128)(2,1)}), bf16[8,128,1152]{2,1,0:T(8,128)(2,1)}, u32[]{:S(2)}, u32[]{:S(2)}) async-start(bf16[8,128,1152]{2,1,0:T(8,128)(2,1)} %bitcast.130), calls=%async_computation.1 | async-start | bytes 4718592 | tf_op jit(solution)/shard_map/all_to_all | solution.py:46
  337.3 66.2 %all-gather.17.cloned.1.call-start = ((), (), s32[]{:S(2)}) async-start(), calls=%async_computation.17 | async-start | bytes 2654208 | tf_op jit(solution)/shard_map/all_gather | solution.py:205
  376.8 127.2 %reduce-scatter.7.cloned.1.call-start = ((), (), s32[]{:S(2)}) async-start(), calls=%async_computation.18 | async-start | bytes 2654208 | tf_op jit(solution)/shard_map/reduce_scatter | solution.py:261
  419.0 31.8 %copy-start.46 = (s32[1152]{0:T(1024)S(1)}, s32[1152]{0:T(1024)}, u32[]{:S(2)}) copy-start(s32[1152]{0:T(1024)} %fusion.83) | copy-start | bytes 13828
  458.5 145.3 %reduce-scatter.13.cloned.1.call-start = ((), (), s32[]{:S(2)}) async-start(), calls=%async_computation.22 | async-start | bytes 2488320
  486.6 56.4 %all-to-all-start.3 = ((bf16[8,512,512]{2,1,0:T(8,128)(2,1)}), bf16[8,512,512]{2,1,0:T(8,128)(2,1)}, u32[]{:S(2)}, u32[]{:S(2)}) async-start(bf16[8,512,512]{2,1,0:T(8,128)(2,1)} %bitcast.122), calls=%async_computation.3 | async-start | bytes 8388608 | tf_op jit(solution)/shard_map/all_to_all | solution.py:46
  491.2 114.7 %reduce-scatter.9.cloned.1.call-start = ((), (), s32[]{:S(2)}) async-start(), calls=%async_computation.19 | async-start | bytes 368640 | tf_op jit(solution)/shard_map/reduce_scatter | solution.py:262
  504.1 147.3 %reduce-scatter.11.cloned.1.call-start = ((), (), s32[]{:S(2)}) async-start(), calls=%async_computation.20 | async-start | bytes 5160960 | tf_op jit(solution)/shard_map/reduce_scatter | solution.py:213
  520.4 38.2 %copy-start.40 = (f32[128,4]{0,1:T(4,128)S(1)}, f32[128,4]{0,1:T(4,128)}, u32[]{:S(2)}) copy-start(f32[128,4]{0,1:T(4,128)} %copy-done.39) | copy-start | bytes 6148
  546.8 22.4 %all-to-all-start.4 = ((bf16[4,128,512]{2,1,0:T(8,128)(2,1)}), bf16[4,128,512]{2,1,0:T(8,128)(2,1)}, u32[]{:S(2)}, u32[]{:S(2)}) async-start(bf16[4,128,512]{2,1,0:T(8,128)(2,1)} %bitcast.26), calls=%async_computation.4 | async-start | bytes 1048576 | tf_op jit(solution)/shard_map/all_to_all | solution.py:46
  581.8 18.2 %all-to-all-start.5 = ((f32[32,1,160]{2,1,0:T(1,128)}), f32[32,1,160]{2,1,0:T(1,128)}, u32[]{:S(2)}, u32[]{:S(2)}) async-start(f32[32,1,160]{2,1,0:T(1,128)} %all_to_all.35), calls=%async_computation.5 | async-start | bytes 65536 | tf_op jit(solution)/shard_map/all_to_all | solution.py:290
  600.0 53.5 %all-to-all-start.6 = ((bf16[8,144,1536]{2,1,0:T(8,128)(2,1)}), bf16[8,144,1536]{2,1,0:T(8,128)(2,1)S(1)}, u32[]{:S(2)}, u32[]{:S(2)}) async-start(bf16[8,144,1536]{2,1,0:T(8,128)(2,1)} %reshape.536), calls=%async_computation.6 | async-start | bytes 7077888 | tf_op jit(solution)/shard_map/all_to_all | solution.py:46
  603.8 54.2 %copy-start.55 = (f32[128]{0:T(128)S(1)}, f32[128]{0:T(128)}, u32[]{:S(2)}) copy-start(f32[128]{0:T(128)} %rsqrt.73) | copy-start | bytes 1540
  653.5 20.4 %all-to-all-start.8 = ((bf16[8,36,1792]{2,1,0:T(8,128)(2,1)}), bf16[8,36,1792]{2,1,0:T(8,128)(2,1)}, u32[]{:S(2)}, u32[]{:S(2)}) async-start(bf16[8,36,1792]{2,1,0:T(8,128)(2,1)} %reshape.525), calls=%async_computation.11 | async-start | bytes 2293760 | tf_op jit(solution)/shard_map/all_to_all | solution.py:269
  673.9 17.8 %all-to-all-start.7 = ((bf16[4,36,1536]{2,1,0:T(8,128)(2,1)}), bf16[4,36,1536]{2,1,0:T(8,128)(2,1)S(1)}, u32[]{:S(2)}, u32[]{:S(2)}) async-start(bf16[4,36,1536]{2,1,0:T(8,128)(2,1)} %convert_element_type.238), calls=%async_computation.7 | async-start | bytes 983040 | tf_op jit(solution)/shard_map/all_to_all | solution.py:46
  (57 other events, 318.1 us)
Sparse Core Ops, SparseCore 0:
  12.9 74.6 all-gather.18
  108.1 62.4 all-gather.8
  172.8 78.2 all-gather.12
  253.3 27.5 all-gather.10
  282.4 43.9 all-gather.14
  376.9 26.5 all-gather.16
  458.6 45.3 reduce-scatter.6
  506.4 45.0 reduce-scatter.12
  553.9 19.7 reduce-scatter.8
  576.0 75.2 reduce-scatter.10

commit v2 on v1

--- a/solution.py
+++ b/solution.py
@@ -111,6 +111,13 @@
         [w_query, w_key, w_value, gains_own, w_output.reshape(wrows, qwidth)], axis=1
     )
     packed = lax.all_gather(pack, everyone, axis=0, tiled=False)
+    def by_rank(weight):
+        cut = weight.reshape(wrows, S, Z, X, units).transpose(1, 3, 0, 2, 4)
+        return jnp.pad(cut.reshape(ranks, wrows, mine), ((0, 0), (0, 0), (0, padded - mine)))
+
+    sent = jnp.concatenate([by_rank(w_gate), by_rank(w_up)], axis=2)
+    arrived = lax.all_to_all(sent, group, split_axis=0, concat_axis=0, tiled=True)
+    packed, arrived = lax.optimization_barrier((packed, arrived))
     qkv_weight = packed[:, :, :qkv_width].reshape(width, qkv_width)
     output_weight = packed[:, :, qkv_width + 128 :].reshape(qwidth, width)
     gain_block = packed[:, :, qkv_width : qkv_width + 8].astype(full)
@@ -121,12 +128,6 @@
         gain_block[:, : norm_query.shape[0], i].reshape(head_dim) for i in (4, 5)
     )
 
-    def by_rank(weight):
-        cut = weight.reshape(wrows, S, Z, X, units).transpose(1, 3, 0, 2, 4)
-        return jnp.pad(cut.reshape(ranks, wrows, mine), ((0, 0), (0, 0), (0, padded - mine)))
-
-    sent = jnp.concatenate([by_rank(w_gate), by_rank(w_up)], axis=2)
-    arrived = lax.all_to_all(sent, group, split_axis=0, concat_axis=0, tiled=True)
     hidden_weight = lax.all_gather(
         arrived.reshape(ranks * wrows, 2 * padded), "wz", axis=0, tiled=True
     )
@@ -163,6 +164,7 @@
     value_raw = qkv_raw[:, qwidth + head_dim :]
     key_shaped, key_pull = jax.vjp(key_side, key_raw, gain_key)
     kv_own = jnp.concatenate([key_shaped, value_raw], axis=1).astype(low)
+    kv_own, hidden_weight = lax.optimization_barrier((kv_own, hidden_weight))
     all_kv = lax.all_gather(
         kv_own.reshape(seqs, rows, 2 * head_dim), everyone, axis=1, tiled=True
     )
@@ -207,12 +209,12 @@
     d_gate, d_up = middle_pull(d_middle)
     d_hidden = jnp.concatenate([d_gate.astype(low), d_up.astype(low)], axis=1)
     d_shuffled = spread_sum(dot_t(d_hidden, hidden_weight).reshape(ranks, own, width), group)
-    grad_down = lax.psum_scatter(
-        t_dot(middle, d_output).astype(low), "wz", scatter_dimension=0, tiled=True
-    ).astype(full)
     grad_hidden = lax.psum_scatter(
         t_dot(normed_all, d_hidden).astype(low), "wz", scatter_dimension=0, tiled=True
     )
+    down_part = t_dot(middle, d_output).astype(low)
+    down_part, grad_hidden = lax.optimization_barrier((down_part, grad_hidden))
+    grad_down = lax.psum_scatter(down_part, "wz", scatter_dimension=0, tiled=True)
     coarse = d_shuffled.astype(low)
     fine = (d_shuffled - coarse.astype(full)).astype(low)
     d_normed_ffw = dot_t(coarse, shuffle) + dot_t(fine, shuffle)
@@ -258,6 +260,7 @@
 
     out_blocks = t_dot(token_heads, d_branch).astype(low).reshape(S, Z, X, orows, width)
     out_blocks = out_blocks.transpose(0, 2, 1, 3, 4).reshape(qwidth, width)
+    out_blocks, grad_down = lax.optimization_barrier((out_blocks, grad_down))
     out_part = lax.psum_scatter(out_blocks, group, scatter_dimension=0, tiled=True)
     grad_output = lax.psum_scatter(out_part, "wz", scatter_dimension=0, tiled=True).astype(full)
 
@@ -309,7 +312,7 @@
         gains[4],
         grad_gate,
         grad_upward,
-        grad_down,
+        grad_down.astype(full),
         gains[5],
     )
 

time: 709 us -> 716 us (level)
  waiting for transfers between devices: 365 us -> 406 us
  blocking collectives: 53.9 us -> 22.5 us
    all_to_all x5 -> x6, waiting for transfers between devices: 60.1 us -> 121 us  [spread_sum(): lax.all_to_all(parts.astype(jnp.bfloat16), axes, split_axis=0, concat_axi...]
    all_gather x1, waiting for transfers between devices: 14.1 us -> 49 us  [on_device(): lax.all_gather(kv_own.reshape(seqs, rows, 2 * head_dim), everyone, axis=1...]
    all_to_all x1 -> x0, blocking collectives: 31.5 us -> none  [spread_sum(): lax.all_to_all(parts.astype(jnp.bfloat16), axes, split_axis=0, concat_axi...]
    reduce_scatter x1, waiting for transfers between devices: 43.3 us -> 17.8 us  [on_device(): lax.psum_scatter(t_dot(normed_all, d_hidden).astype(low), 'wz', scatter_d...]
    all_gather x1, waiting for transfers between devices: 72.2 us -> 48.5 us  [on_device(): packed = lax.all_gather(pack, everyone, axis=0, tiled=False)]
    reduce_scatter x1, waiting for transfers between devices: 12.8 us -> 0.01 us  [on_device(): lax.psum_scatter(out_blocks, group, scatter_dimension=0, tiled=True)]
    reduce_scatter x1, waiting for transfers between devices: 0.01 us -> 9.86 us  [on_device(): lax.psum_scatter(out_part, 'wz', scatter_dimension=0, tiled=True)]
    all_to_all x5 -> x6, starting transfers between devices: 21.7 us -> 26.9 us  [spread_sum(): lax.all_to_all(parts.astype(jnp.bfloat16), axes, split_axis=0, concat_axi...]
  transfers between devices with their start and end apart: 17 -> 18, of which waited for: 13 -> 15; matrix products, arithmetic and copies ran while one was open for 23% -> 23% of each run, Pallas kernels for 0% -> 0%
where the time goes in v2:
time: 716 us; the launch traced here: 708 us
  waiting for transfers between devices  406 us (57%)
  local copies, waits for them, and re-layouts  101 us (14%)
  matrix products  73 us (10%)
  other arithmetic  53.6 us (7%)
  starting transfers between devices  36.6 us (5%)
  blocking collectives  22.5 us (3%)
  between operations  15.8 us (2%)
    all_to_all x6, waiting for transfers between devices, spread_sum(): lax.all_to_all(parts.astype(jnp.bfloat16), axes, split_axis=0, concat_axi...  121 us
    all_gather x1, waiting for transfers between devices, on_device(): lax.all_gather(arrived.reshape(ranks * wrows, 2 * padded), 'wz', axis=0,...  61.8 us
    all_gather x1, waiting for transfers between devices, on_device(): lax.all_gather(kv_own.reshape(seqs, rows, 2 * head_dim), everyone, axis=1...  49 us
    all_gather x1, waiting for transfers between devices, on_device(): packed = lax.all_gather(pack, everyone, axis=0, tiled=False)  48.5 us
    all_gather x1, waiting for transfers between devices, on_device(): down_weight = lax.all_gather(w_down, 'wz', axis=0, tiled=True)  33.1 us
    all_gather x1, waiting for transfers between devices, on_device(): normed_all = lax.all_gather(normed_ffw, group, axis=0, tiled=True)  27.1 us
    all_to_all x6, starting transfers between devices, spread_sum(): lax.all_to_all(parts.astype(jnp.bfloat16), axes, split_axis=0, concat_axi...  26.9 us
    all_gather x1, waiting for transfers between devices, on_device(): d_output = lax.all_gather(d_output_f.astype(low), group, axis=0, tiled=True)  26.8 us
  transfers between devices with their start and end apart: 18, of which 15 were waited for; matrix products, arithmetic and copies ran while one was open for 23% of the time, Pallas kernels for 0%

profile of v2, /device:TPU:0, one launch (start us, length us, event | category | flops | bytes accessed | tf_op | source)
XLA Modules:
  0.0 708.0 jit_solution(12587578797964998458)
XLA Ops:
  19.3 22.5 %all_to_all.49 = bf16[8,36,1792]{2,1,0:T(8,128)(2,1)S(1)} all-to-all(bf16[8,36,1792]{2,1,0:T(8,128)(2,1)S(1)} %copy.117), channel_id=1, replica_groups=mesh['seq'=4,'wz'=4,'wx'=2] {'seq','wx'}, dimensions={0} | all-to-all | bytes 2064384 | tf_op jit(solution)/shard_map/all_to_all | solution.py:119
  41.7 48.5 %all-gather.19.cloned.1.call-done = bf16[32,36,2688]{2,1,0:T(8,128)(2,1)} async-done(((bf16[1,36,2688]{2,1,0:T(8,128)(2,1)}), bf16[32,36,2688]{2,1,0:T(8,128)(2,1)}) %all-gather.19.cloned.1.call-update) | async-done | bytes 6193168 | tf_op jit(solution)/shard_map/all_gather | solution.py:113
  108.9 61.8 %all-gather.9.cloned.1.call-done = bf16[1152,1792]{1,0:T(8,128)(2,1)} async-done(((bf16[288,1792]{1,0:T(8,128)(2,1)}), bf16[1152,1792]{1,0:T(8,128)(2,1)}) %all-gather.9.cloned.1.call-update) | async-done | bytes 4128784 | tf_op jit(solution)/shard_map/all_gather | solution.py:131
  185.8 49.0 %all-gather.11.cloned.1.call-done = bf16[2,2048,512]{2,1,0:T(8,128)(2,1)} async-done(((bf16[2,64,512]{2,1,0:T(8,128)(2,1)}), bf16[2,2048,512]{2,1,0:T(8,128)(2,1)}) %all-gather.11.cloned.1.call-update) | async-done | bytes 4194320 | tf_op jit(solution)/shard_map/all_gather | solution.py:168
  234.8 5.3 fusion.114
  250.5 27.1 %all-gather.13.cloned.1.call-done = bf16[1024,1152]{1,0:T(8,128)(2,1)} async-done(((bf16[128,1152]{1,0:T(8,128)(2,1)}), bf16[1024,1152]{1,0:T(8,128)(2,1)}) %all-gather.13.cloned.1.call-update) | async-done | bytes 2359312 | tf_op jit(solution)/shard_map/all_gather | solution.py:196
  277.6 7.8 %fusion.118 = f32[1024,1792]{1,0:T(8,128)S(1)} fusion(bf16[1024,1152]{1,0:T(8,128)(2,1)} %all-gather.13.cloned.1.call-done, bf16[1152,1792]{1,0:T(8,128)(2,1)} %all-gather.9.cloned.1.call-done), kind=kOutput, calls=%fused_computation.239 | convolution fusion | flops 4227858432 | bytes 13828096 | tf_op jit(solution)/shard_map/dot_general | solution.py:90
  289.9 33.1 %all-gather.15.cloned.1.call-done = bf16[864,1152]{1,0:T(8,128)(2,1)} async-done(((bf16[216,1152]{1,0:T(8,128)(2,1)}), bf16[864,1152]{1,0:T(8,128)(2,1)}) %all-gather.15.cloned.1.call-update) | async-done | bytes 1990672 | tf_op jit(solution)/shard_map/all_gather | solution.py:134
  323.1 6.4 convolution_convert_fusion.4
  335.3 27.8 %all-to-all-done.1 = bf16[8,128,1152]{2,1,0:T(8,128)(2,1)} async-done(((bf16[8,128,1152]{2,1,0:T(8,128)(2,1)}), bf16[8,128,1152]{2,1,0:T(8,128)(2,1)}, u32[]{:S(2)}, u32[]{:S(2)}) %all-to-all-start.1) | async-done | bytes 2359328 | tf_op jit(solution)/shard_map/all_to_all | solution.py:46
  373.5 26.8 %all-gather.17.cloned.1.call-done = bf16[1024,1152]{1,0:T(8,128)(2,1)} async-done(((bf16[128,1152]{1,0:T(8,128)(2,1)}), bf16[1024,1152]{1,0:T(8,128)(2,1)}) %all-gather.17.cloned.1.call-update) | async-done | bytes 2359312 | tf_op jit(solution)/shard_map/all_gather | solution.py:207
  405.3 5.1 fusion.11
  410.5 6.2 convolution_convert_fusion.3
  421.3 9.2 %convolution_convert_fusion = bf16[1152,1792]{1,0:T(8,128)(2,1)} fusion(bf16[1024,1152]{1,0:T(8,128)(2,1)} %all-gather.13.cloned.1.call-done, bf16[1024,896]{1,0:T(8,128)(2,1)} %copy-done.17, bf16[1024,896]{1,0:T(8,128)(2,1)} %copy-done.16), kind=kOutput, calls=%fused_computation.1 | convolution fusion | flops 4237262848 | bytes 10158080 | tf_op jit(solution)/shard_map/nd,nc->dc/dot_general | solution.py:96
  430.5 19.5 %all-to-all-done.2 = bf16[8,128,1152]{2,1,0:T(8,128)(2,1)} async-done(((bf16[8,128,1152]{2,1,0:T(8,128)(2,1)}), bf16[8,128,1152]{2,1,0:T(8,128)(2,1)}, u32[]{:S(2)}, u32[]{:S(2)}) %all-to-all-start.2) | async-done | bytes 2359328 | tf_op jit(solution)/shard_map/all_to_all | solution.py:46
  468.2 6.3 copy.125
  484.0 6.0 convolution_convert_fusion.5
  490.0 17.8 %reduce-scatter.7.cloned.1.call-done = bf16[288,1792]{1,0:T(8,128)(2,1)} async-done(((bf16[1152,1792]{1,0:T(8,128)(2,1)}), bf16[288,1792]{1,0:T(8,128)(2,1)}) %reduce-scatter.7.cloned.1.call-update) | async-done | bytes 1032208 | tf_op jit(solution)/shard_map/reduce_scatter | solution.py:212
  513.7 18.8 %all-to-all-done.3 = bf16[8,512,512]{2,1,0:T(8,128)(2,1)} async-done(((bf16[8,512,512]{2,1,0:T(8,128)(2,1)}), bf16[8,512,512]{2,1,0:T(8,128)(2,1)}, u32[]{:S(2)}, u32[]{:S(2)}) %all-to-all-start.3) | async-done | bytes 4194336 | tf_op jit(solution)/shard_map/all_to_all | solution.py:46
  553.1 9.8 %all-to-all-done.4 = bf16[4,128,512]{2,1,0:T(8,128)(2,1)} async-done(((bf16[4,128,512]{2,1,0:T(8,128)(2,1)}), bf16[4,128,512]{2,1,0:T(8,128)(2,1)}, u32[]{:S(2)}, u32[]{:S(2)}) %all-to-all-start.4) | async-done | bytes 524320 | tf_op jit(solution)/shard_map/all_to_all | solution.py:46
  588.5 5.7 reshape.533
  604.5 41.5 %all-to-all-done.6 = bf16[8,144,1536]{2,1,0:T(8,128)(2,1)S(1)} async-done(((bf16[8,144,1536]{2,1,0:T(8,128)(2,1)}), bf16[8,144,1536]{2,1,0:T(8,128)(2,1)S(1)}, u32[]{:S(2)}, u32[]{:S(2)}) %all-to-all-start.6) | async-done | bytes 3538976 | tf_op jit(solution)/shard_map/all_to_all | solution.py:46
  657.8 11.2 %all-to-all-done.8 = bf16[8,36,1792]{2,1,0:T(8,128)(2,1)} async-done(((bf16[8,36,1792]{2,1,0:T(8,128)(2,1)}), bf16[8,36,1792]{2,1,0:T(8,128)(2,1)}, u32[]{:S(2)}, u32[]{:S(2)}) %all-to-all-start.8) | async-done | bytes 1032224 | tf_op jit(solution)/shard_map/all_to_all | solution.py:272
  689.3 9.9 %reduce-scatter.11.cloned.1.call-done = bf16[32,1152]{1,0:T(8,128)(2,1)} async-done(((bf16[128,1152]{1,0:T(8,128)(2,1)}), bf16[32,1152]{1,0:T(8,128)(2,1)}) %reduce-scatter.11.cloned.1.call-update) | async-done | bytes 73744 | tf_op jit(solution)/shard_map/reduce_scatter | solution.py:265
  (309 shorter events, 209.4 us)
Async XLA Ops:
  7.2 83.1 %all-gather.19.cloned.1.call-start = ((), (), s32[]{:S(2)}) async-start(), calls=%async_computation.21 | async-start | bytes 7096320 | tf_op jit(solution)/shard_map/all_gather | solution.py:113
  12.9 157.8 %all-gather.9.cloned.1.call-start = ((), (), s32[]{:S(2)}) async-start(), calls=%async_computation.13 | async-start | bytes 5160960 | tf_op jit(solution)/shard_map/all_gather | solution.py:131
  19.1 72.4 %copy-start.8 = (bf16[2,64,1152]{2,1,0:T(8,128)(2,1)S(1)}, bf16[2,64,1152]{2,1,0:T(8,128)(2,1)}, u32[]{:S(2)}) copy-start(bf16[2,64,1152]{2,1,0:T(8,128)(2,1)} %param.15) | copy-start | bytes 884740
  91.3 143.5 %all-gather.11.cloned.1.call-start = ((), (), s32[]{:S(2)}) async-start(), calls=%async_computation.14 | async-start | bytes 4325376 | tf_op jit(solution)/shard_map/all_gather | solution.py:168
  105.1 71.2 %copy-start.1 = (bf16[1152,1536]{1,0:T(8,128)(2,1)}, bf16[1152,1536]{1,0:T(8,128)(2,1)S(1)}, u32[]{:S(2)}) copy-start(bf16[1152,1536]{1,0:T(8,128)(2,1)S(1)} %reshape.500) | copy-start | bytes 10616836
  108.1 68.2 %copy-start.50 = (f32[128]{0:T(128)}, f32[128]{0:T(128)S(1)}, u32[]{:S(2)}) copy-start(f32[128]{0:T(128)S(1)} %fusion.94) | copy-start | bytes 1540
  170.7 107.0 %all-gather.13.cloned.1.call-start = ((), (), s32[]{:S(2)}) async-start(), calls=%async_computation.15 | async-start | bytes 2654208 | tf_op jit(solution)/shard_map/all_gather | solution.py:196
  184.3 55.8 %copy-start.3 = (f32[128,4,256]{2,1,0:T(4,128)}, f32[128,4,256]{2,1,0:T(4,128)S(1)}, u32[]{:S(2)}) copy-start(f32[128,4,256]{2,1,0:T(4,128)S(1)} %reshape.501) | copy-start | bytes 1572868
  184.6 55.5 %copy-start.40 = (f32[128,4]{0,1:T(4,128)}, f32[128,4]{0,1:T(4,128)S(1)}, u32[]{:S(2)}) copy-start(f32[128,4]{0,1:T(4,128)S(1)} %copy.118) | copy-start | bytes 6148
  184.7 55.4 %copy-start.18 = (f32[128,4]{1,0:T(8,128)}, f32[128,4]{1,0:T(8,128)S(1)}, u32[]{:S(2)}) copy-start(f32[128,4]{1,0:T(8,128)S(1)} %copy.119) | copy-start | bytes 6148
  249.9 73.2 %all-gather.15.cloned.1.call-start = ((), (), s32[]{:S(2)}) async-start(), calls=%async_computation.16 | async-start | bytes 2488320 | tf_op jit(solution)/shard_map/all_gather | solution.py:134
  329.5 33.5 %all-to-all-start.1 = ((bf16[8,128,1152]{2,1,0:T(8,128)(2,1)}), bf16[8,128,1152]{2,1,0:T(8,128)(2,1)}, u32[]{:S(2)}, u32[]{:S(2)}) async-start(bf16[8,128,1152]{2,1,0:T(8,128)(2,1)} %bitcast.129), calls=%async_computation.1 | async-start | bytes 4718592 | tf_op jit(solution)/shard_map/all_to_all | solution.py:46
  334.0 66.2 %all-gather.17.cloned.1.call-start = ((), (), s32[]{:S(2)}) async-start(), calls=%async_computation.17 | async-start | bytes 2654208 | tf_op jit(solution)/shard_map/all_gather | solution.py:207
  416.7 33.3 %all-to-all-start.2 = ((bf16[8,128,1152]{2,1,0:T(8,128)(2,1)}), bf16[8,128,1152]{2,1,0:T(8,128)(2,1)}, u32[]{:S(2)}, u32[]{:S(2)}) async-start(bf16[8,128,1152]{2,1,0:T(8,128)(2,1)} %bitcast.128), calls=%async_computation.2 | async-start | bytes 4718592 | tf_op jit(solution)/shard_map/all_to_all | solution.py:46
  421.1 86.7 %reduce-scatter.7.cloned.1.call-start = ((), (), s32[]{:S(2)}) async-start(), calls=%async_computation.18 | async-start | bytes 5160960 | tf_op jit(solution)/shard_map/reduce_scatter | solution.py:212
  479.1 53.4 %all-to-all-start.3 = ((bf16[8,512,512]{2,1,0:T(8,128)(2,1)}), bf16[8,512,512]{2,1,0:T(8,128)(2,1)}, u32[]{:S(2)}, u32[]{:S(2)}) async-start(bf16[8,512,512]{2,1,0:T(8,128)(2,1)} %bitcast.120), calls=%async_computation.3 | async-start | bytes 8388608 | tf_op jit(solution)/shard_map/all_to_all | solution.py:46
  483.9 117.6 %reduce-scatter.13.cloned.1.call-start = ((), (), s32[]{:S(2)}) async-start(), calls=%async_computation.22 | async-start | bytes 2488320
  536.2 26.7 %all-to-all-start.4 = ((bf16[4,128,512]{2,1,0:T(8,128)(2,1)}), bf16[4,128,512]{2,1,0:T(8,128)(2,1)}, u32[]{:S(2)}, u32[]{:S(2)}) async-start(bf16[4,128,512]{2,1,0:T(8,128)(2,1)} %bitcast.24), calls=%async_computation.4 | async-start | bytes 1048576 | tf_op jit(solution)/shard_map/all_to_all | solution.py:46
  575.5 18.6 %all-to-all-start.5 = ((f32[32,1,160]{2,1,0:T(1,128)}), f32[32,1,160]{2,1,0:T(1,128)}, u32[]{:S(2)}, u32[]{:S(2)}) async-start(f32[32,1,160]{2,1,0:T(1,128)} %all_to_all.35), calls=%async_computation.5 | async-start | bytes 65536 | tf_op jit(solution)/shard_map/all_to_all | solution.py:293
  594.1 51.8 %all-to-all-start.6 = ((bf16[8,144,1536]{2,1,0:T(8,128)(2,1)}), bf16[8,144,1536]{2,1,0:T(8,128)(2,1)S(1)}, u32[]{:S(2)}, u32[]{:S(2)}) async-start(bf16[8,144,1536]{2,1,0:T(8,128)(2,1)} %reshape.533), calls=%async_computation.6 | async-start | bytes 7077888 | tf_op jit(solution)/shard_map/all_to_all | solution.py:46
  598.0 81.4 %reduce-scatter.9.cloned.1.call-start = ((), (), s32[]{:S(2)}) async-start(), calls=%async_computation.19 | async-start | bytes 2654208 | tf_op jit(solution)/shard_map/reduce_scatter | solution.py:264
  646.0 23.0 %all-to-all-start.8 = ((bf16[8,36,1792]{2,1,0:T(8,128)(2,1)}), bf16[8,36,1792]{2,1,0:T(8,128)(2,1)}, u32[]{:S(2)}, u32[]{:S(2)}) async-start(bf16[8,36,1792]{2,1,0:T(8,128)(2,1)} %reshape.522), calls=%async_computation.11 | async-start | bytes 2293760 | tf_op jit(solution)/shard_map/all_to_all | solution.py:272
  669.0 17.9 %all-to-all-start.7 = ((bf16[4,36,1536]{2,1,0:T(8,128)(2,1)}), bf16[4,36,1536]{2,1,0:T(8,128)(2,1)S(1)}, u32[]{:S(2)}, u32[]{:S(2)}) async-start(bf16[4,36,1536]{2,1,0:T(8,128)(2,1)} %convert_element_type.237), calls=%async_computation.7 | async-start | bytes 983040 | tf_op jit(solution)/shard_map/all_to_all | solution.py:46
  673.6 25.6 %reduce-scatter.11.cloned.1.call-start = ((), (), s32[]{:S(2)}) async-start(), calls=%async_computation.20 | async-start | bytes 368640 | tf_op jit(solution)/shard_map/reduce_scatter | solution.py:265
  (60 other events, 574.7 us)
Sparse Core Ops, SparseCore 0:
  13.0 77.2 all-gather.18
  92.4 78.1 all-gather.8
  174.3 60.5 all-gather.10
  250.0 27.5 all-gather.12
  279.1 43.9 all-gather.14
  373.6 26.5 all-gather.16
  430.7 77.0 reduce-scatter.6
  510.2 47.7 reduce-scatter.12
  602.6 57.2 reduce-scatter.8
  679.6 19.6 reduce-scatter.10
